TPU v7x, 256 devices: a whole 4x4x8 slice. The times are simulated.
256 devices in a mesh: node: 32 (over y_hi, z, core), local: 8 (over y_lo, x).
Axes of the slice: x: 4, y: 4 (y_hi: 2, y_lo: 2; y = y_hi * 2 + y_lo), z: 8, core: 2. Of those that a mesh axis runs over, the one named last changes fastest.
Arguments:
- hidden_acts: bfloat16 [262144, 1024], P(('node', 'local')), may hold values from -6 to 6
- out_grad: bfloat16 [262144, 4096], P(('node', 'local')), may hold values from -1.5 to 1.5
- live_counts: int32 [32, 8], P('node', 'local'), may hold values from 256 to 1024, as said below
- master: float32 [1024, 4096], P('local', 'node'), may hold values from -2.5 to 2.5
- first: float32 [1024, 4096], P('local', 'node'), may hold values from -15 to 15
- second: float32 [1024, 4096], P('local', 'node'), may hold values from 1 to 100
Outputs:
- new_master: float32 [1024, 4096], P('local', 'node')
- new_first: float32 [1024, 4096], P('local', 'node')
- new_second: float32 [1024, 4096], P('local', 'node')
- weights_next: bfloat16 [1024, 4096], P('local')
Inputs may be any that keep to these rules, and one draw needn't show every extreme that they name: `live_counts`: both ends are reached on some device in every draw.
All inputs are finite; a program needn't handle non-finite values.
Results may differ from a plain program's by a relative error of at most 0.001.
Values may be sent and summed in bfloat16 or wider, within the bound.
A program may use at most 128 MiB of HBM per device.

v0:
```python
import jax
import jax.numpy as jnp
from jax import lax
from jax.sharding import PartitionSpec as P

ADAM_STEP = 10


def body(hidden_acts, out_grad, live_counts, master, first, second):
    slots = hidden_acts.shape[0]
    live = live_counts[0, 0]
    keep = (lax.iota(jnp.int32, slots) < live)[:, None]
    masked = jnp.where(keep, out_grad, jnp.zeros_like(out_grad))
    partial_sum = lax.psum_scatter(
        lax.dot_general(
            masked, hidden_acts, (((0,), (0,)), ((), ())), preferred_element_type=jnp.float32
        ),
        "node",
        scatter_dimension=0,
        tiled=True,
    )
    owned = lax.psum_scatter(partial_sum, "local", scatter_dimension=1, tiled=True)
    grad = owned.T
    new_first = 0.9 * first + 0.1 * grad
    new_second = 0.95 * second + 0.05 * grad * grad
    update = (
        new_first
        / (1.0 - 0.9**ADAM_STEP)
        / (jnp.sqrt(new_second / (1.0 - 0.95**ADAM_STEP)) + 1e-08)
    )
    new_master = master - 0.02 * (update + 0.1 * master)
    weights_next = lax.all_gather(new_master.astype(jnp.bfloat16), "node", axis=1, tiled=True)
    return (new_master, new_first, new_second, weights_next)


def solution(mesh):
    in_specs = (
        P(("node", "local"), None),
        P(("node", "local"), None),
        P("node", "local"),
        P("local", "node"),
        P("local", "node"),
        P("local", "node"),
    )
    out_specs = (P("local", "node"), P("local", "node"), P("local", "node"), P("local", None))
    return jax.shard_map(body, mesh=mesh, in_specs=in_specs, out_specs=out_specs, check_vma=False)
```

profile of v0, /device:TPU:1, one launch (start us, length us, event | category | flops | bytes accessed | tf_op | source)
XLA Modules:
  0.0 377.6 jit_solution(16929709773293093539)
XLA Ops:
  7.2 0.0 copy-start
  7.2 0.0 reduce-scatter.3.cloned.1.call-start
  8.0 0.8 copy-done
  8.8 14.8 %fusion = f32[4096,1024]{1,0:T(8,128)} fusion(bf16[1024,1024]{1,0:T(8,128)(2,1)S(1)} %copy-done, bf16[1024,4096]{1,0:T(8,128)(2,1)} %param.7, pred[1024]{0:T(1024)(128)(4,1)S(1)} %iota_compare_fusion), kind=kOutput, calls=%fused_computation | convolution fusion | flops 8594128896 | bytes 27264000 | tf_op jit(solution)/shard_map/dot_general | solution.py:15
  23.6 0.0 copy-start.1
  23.6 0.0 copy-start.2
  23.6 0.0 copy-start.3
  23.6 0.0 reduce-scatter.3.cloned.1.call-update
  23.6 0.0 reduce-scatter.5.cloned.1.call-start
  23.7 219.9 %reduce-scatter.3.cloned.1.call-done = f32[128,1024]{1,0:T(8,128)} async-done(((f32[4096,1024]{1,0:T(8,128)}), f32[128,1024]{1,0:T(8,128)}) %reduce-scatter.3.cloned.1.call-update) | async-done | bytes 524304 | tf_op jit(solution)/shard_map/reduce_scatter | solution.py:14
  243.6 0.0 reduce-scatter.5.cloned.1.call-update
  243.6 0.0 all-gather.2.cloned.1.call-start
  243.7 0.0 copy-done.1
  243.7 0.1 copy.10
  243.8 0.0 copy-done.2
  243.8 0.1 copy.11
  243.9 0.0 copy-done.3
  243.9 0.1 copy.13
  244.0 39.6 %reduce-scatter.5.cloned.1.call-done = f32[128,128]{1,0:T(8,128)} async-done(((f32[128,1024]{1,0:T(8,128)}), f32[128,128]{1,0:T(8,128)}) %reduce-scatter.5.cloned.1.call-update) | async-done | bytes 65552 | tf_op jit(solution)/shard_map/reduce_scatter | solution.py:22
  283.6 1.5 fusion.7
  285.1 0.0 all-gather.2.cloned.1.call-update
  285.2 0.7 copy.14
  285.9 0.7 copy.15
  286.6 0.7 copy.16
  287.3 81.5 %all-gather.2.cloned.1.call-done = bf16[128,4096]{0,1:T(8,128)(2,1)} async-done(((bf16[128,128]{0,1:T(8,128)(2,1)}), bf16[128,4096]{0,1:T(8,128)(2,1)}) %all-gather.2.cloned.1.call-update) | async-done | bytes 1048592 | tf_op jit(solution)/shard_map/all_gather | solution.py:32
  368.8 2.3 copy.17
  (1 shorter events, 0.0 us)
Async XLA Ops:
  7.2 1.6 copy-start
  7.2 236.4 %reduce-scatter.3.cloned.1.call-start = ((), (), s32[]{:S(2)}) async-start(), calls=%async_computation.2 | async-start | bytes 17301504 | tf_op jit(solution)/shard_map/reduce_scatter | solution.py:14
  23.6 220.1 %copy-start.1 = (f32[128,128]{1,0:T(8,128)S(1)}, f32[128,128]{1,0:T(8,128)}, u32[]{:S(2)}) copy-start(f32[128,128]{1,0:T(8,128)} %param.10) | copy-start | bytes 196612
  23.6 220.2 %copy-start.2 = (f32[128,128]{1,0:T(8,128)S(1)}, f32[128,128]{1,0:T(8,128)}, u32[]{:S(2)}) copy-start(f32[128,128]{1,0:T(8,128)} %param.11) | copy-start | bytes 196612
  23.6 220.3 %copy-start.3 = (f32[128,128]{1,0:T(8,128)S(1)}, f32[128,128]{1,0:T(8,128)}, u32[]{:S(2)}) copy-start(f32[128,128]{1,0:T(8,128)} %param.9) | copy-start | bytes 196612
  23.6 260.0 %reduce-scatter.5.cloned.1.call-start = ((), (), s32[]{:S(2)}) async-start(), calls=%async_computation.3 | async-start | bytes 589824 | tf_op jit(solution)/shard_map/reduce_scatter | solution.py:22
  243.6 125.2 %all-gather.2.cloned.1.call-start = ((), (), s32[]{:S(2)}) async-start(), calls=%async_computation.4 | async-start | bytes 1081344 | tf_op jit(solution)/shard_map/all_gather | solution.py:32
Sparse Core Ops, SparseCore 0:
  23.7 219.7 reduce-scatter.2
  246.2 37.3 reduce-scatter.4
  287.0 81.7 all-gather.1
where the time goes:
time: 378 us
  waiting for transfers between devices  341 us (90%)
  matrix products  14.8 us (4%)
  between operations  14.6 us (4%)
  local copies, waits for them, and re-layouts  5.48 us (1%)
    reduce_scatter x1, waiting for transfers between devices, body(): lax.psum_scatter(lax.dot_general(masked, hidden_acts, (((0,), (0,)), ((),...  220 us
    all_gather x1, waiting for transfers between devices, body(): lax.all_gather(new_master.astype(jnp.bfloat16), 'node', axis=1, tiled=True)  81.5 us
    reduce_scatter x1, waiting for transfers between devices, body(): lax.psum_scatter(partial_sum, 'local', scatter_dimension=1, tiled=True)  39.6 us
    dot_general x1, matrix products, body(): lax.dot_general(masked, hidden_acts, (((0,), (0,)), ((), ())), preferred_...  14.8 us
  transfers between devices with their start and end apart: 3, of which 3 were waited for; matrix products, arithmetic and copies ran while one was open for 1% of the time, Pallas kernels for 0%

commit v1 on v0

v1 whole, which is shorter than its diff:
```python
import functools

import jax
import jax.numpy as jnp
from jax import lax
from jax.experimental import pallas as pl
from jax.experimental.pallas import tpu as pltpu
from jax.sharding import PartitionSpec as P

ADAM_STEP = 10
MESH = pl.DeviceIdType.MESH
F32, BF16, I16, I32 = jnp.float32, jnp.bfloat16, jnp.int16, jnp.int32
NX, NY, NZ = 4, 4, 8
TOK, FFW, D = 1024, 1024, 4096
BLK = 128
GROUPS = 4
TOP = 32000.0


def send_codes(load, count, out):
    peak = functools.reduce(jnp.maximum, [jnp.abs(load(i)) for i in range(count)])
    power = jnp.ceil(jnp.log2(jnp.maximum(peak, 1e-30)) * 64.0)
    scale = jnp.exp2(power * (-1.0 / 64.0)) * TOP
    out[0] = power.astype(I32).astype(I16)
    for i in range(count):
        out[i + 1] = jnp.round(load(i) * scale).astype(I32).astype(I16)


def unit_of(message):
    return jnp.exp2(message[0].astype(I32).astype(F32) * (1.0 / 64.0)) * (1.0 / TOP)


def decode(message, i, unit):
    return message[i + 1].astype(I32).astype(F32) * unit


def kernel(
    h_hbm, g_hbm, live_ref, master_ref, first_ref, second_ref,
    new_master_ref, new_first_ref, new_second_ref, w_hbm,
    h_buf, ht, gb, s_buf, a1s, a1r, b1s, b1r, a2s, a2r, b2s, b2r, part, keep2, p2s, p2r, p3s, p3r,
    c1s, c1r, rc, c2s, c2r, kc, c3s, c3r, grad, w_buf,
    h_sem, gl_sem, gs_sem, gr_sem, hs_sem, hr_sem,
    one_s, one_r, two_s, two_r, p2_s, p2_r, p3_s, p3_r, c1_s, c1_r, c2_s, c2_r, c3_s, c3_r,
    wz_s, wz_r, wy_s, wy_r, wc_s, wc_r, wo_sem,
):
    node, local = lax.axis_index("node"), lax.axis_index("local")
    core, z, yh = node % 2, (node // 2) % NZ, node // 16
    x, yl = local % 4, local // 4
    y = yh * 2 + yl

    def dev(dx=0, dy=0, dz=0, dc=0):
        tx, ty, tz, tc = (x + dx) % NX, (y + dy) % NY, (z + dz) % NZ, (core + dc) % 2
        return ((ty // 2) * 16 + tz * 2 + tc, (ty % 2) * 4 + tx)

    def remote(src, dst, send, recv, to):
        return pltpu.make_async_remote_copy(
            src_ref=src, dst_ref=dst, send_sem=send, recv_sem=recv, device_id=to, device_id_type=MESH
        )

    def offset(k):
        return 4 + k // 2 - (k % 2) * (1 + 2 * (k // 2))

    def cols(k, half, c):
        block = half * 16 + ((z + offset(k)) % NZ) * 2 + c
        return pl.ds(pl.multiple_of(block * BLK, BLK), BLK)

    def g_local(k, half):
        return pltpu.make_async_copy(
            g_hbm.at[:, cols(k, half, core)], gb.at[k, pl.ds(0, TOK), pl.ds(half * BLK, BLK)], gl_sem.at[k, half]
        )

    def g_remote(k, half):
        return remote(
            g_hbm.at[:, cols(k, half, 1 - core)], gb.at[k, pl.ds(TOK, TOK), pl.ds(half * BLK, BLK)],
            gs_sem.at[k, half], gr_sem.at[k, half], dev(dc=1),
        )

    def h_load(j):
        return pltpu.make_async_copy(h_hbm.at[:, pl.ds(j * 256, 256)], h_buf.at[:, pl.ds(j * 256, 256)], h_sem.at[j])

    def h_remote(j):
        rows = pl.ds(j * 256, 256)
        return remote(
            ht.at[rows, pl.ds(0, TOK)], ht.at[rows, pl.ds(TOK, TOK)], hs_sem.at[j], hr_sem.at[j], dev(dc=1)
        )

    barrier = pltpu.get_barrier_semaphore()
    partners = [dict(dx=1), dict(dx=2), dict(dx=3), dict(dy=1), dict(dy=2), dict(dy=3), dict(dc=1)]
    partners += [dict(dz=i) for i in range(1, NZ)]
    for partner in partners:
        pl.semaphore_signal(barrier, inc=1, device_id=dev(**partner), device_id_type=MESH)
    for j in range(4):
        h_load(j).start()
    for k in range(8):
        for half in range(2):
            g_local(k, half).start()

    live = live_ref[0, 0]

    def turn(j):
        h_load(j).wait()
        alive = lax.broadcasted_iota(I32, (TOK, 256), 0) < live
        block = jnp.where(alive, h_buf[:, pl.ds(j * 256, 256)].astype(F32), 0.0)
        ht[pl.ds(j * 256, 256), pl.ds(0, TOK)] = block.T.astype(BF16)

    turn(0)
    pl.semaphore_wait(barrier, len(partners))
    for k in range(2):
        for half in range(2):
            g_remote(k, half).start()
    h_remote(0).start()
    for j in range(1, 4):
        turn(j)
        h_remote(j).start()
    for k in range(2, 8):
        for half in range(2):
            g_remote(k, half).start()

    def rows_of(block, start):
        return pl.ds(pl.multiple_of(block * BLK + start, 16), 16)

    def a_tile(g, tx, half, i):
        zi, sub, t = i // 6, (i // 3) % 2, i % 3
        return s_buf[2 * g + zi, half, rows_of(sub * 4 + tx, 16 * t), :]

    def b_tile(g, ty, half, i):
        zi, sub, t = i // 6, (i // 3) % 2, i % 3
        return s_buf[2 * g + zi, ty // 2, rows_of((ty % 2) * 4 + 2 * half + sub, 48 + 16 * t), :]

    def one(axis, g, d):
        src, dst = ((a1s, a1r), (b1s, b1r))[axis]
        step = 1 if d == 0 else 3
        to = dev(dx=step) if axis == 0 else dev(dy=step)
        return remote(src.at[g, d], dst.at[g, d], one_s.at[axis, g, d], one_r.at[axis, g, d], to)

    def two(axis, g, d):
        src, dst = ((a2s, a2r), (b2s, b2r))[axis]
        step = 1 if d == 0 else 3
        to = dev(dx=step) if axis == 0 else dev(dy=step)
        return remote(src.at[g, d], dst.at[g, d], two_s.at[axis, g, d], two_r.at[axis, g, d], to)

    tiles = (a_tile, b_tile)
    here = (x, y)

    def first_hop(axis, g):
        src, tile, me = (a1s, b1s)[axis], tiles[axis], here[axis]
        for d in range(2):
            near = (me + (1 if d == 0 else 3)) % 4
            far = (me + 2) % 4

            def load(i, d=d, near=near, far=far):
                return tile(g, far, d, i) if i < 12 else tile(g, near, 1 - d, i - 12)

            send_codes(load, 24, src.at[g, d])
            one(axis, g, d).start()

    def second_hop(axis, g):
        src, got, tile, me = (a2s, b2s)[axis], (a1r, b1r)[axis], tiles[axis], here[axis]
        for d in range(2):
            one(axis, g, d).wait_recv()
            near = (me + (1 if d == 0 else 3)) % 4
            message = got.at[g, d]
            unit = unit_of(message)

            def load(i, d=d, near=near, message=message, unit=unit):
                return tile(g, near, d, i) + decode(message, i, unit)

            send_codes(load, 12, src.at[g, d])
            two(axis, g, d).start()

    def p2(axis, g, j):
        to = dev(dy=j) if axis == 0 else dev(dx=j)
        return remote(p2s.at[axis, g, j - 1], p2r.at[axis, g, j - 1], p2_s.at[axis, g, j - 1], p2_r.at[axis, g, j - 1], to)

    def second_stage(axis, g):
        direct, relayed, tile, me = (a1r, b1r)[axis], (a2r, b2r)[axis], tiles[axis], here[axis]
        for d in range(2):
            two(axis, g, d).wait_recv()
        for half in range(2):
            far, near = relayed.at[g, half], direct.at[g, 1 - half]
            far_unit, near_unit = unit_of(far), unit_of(near)
            for i in range(12):
                zi, sub, t = i // 6, (i // 3) % 2, i % 3
                total = tile(g, me, half, i) + decode(far, i, far_unit) + decode(near, i + 12, near_unit)
                part[axis, 2 * half + sub, zi * 3 + t] = total
        other = here[1 - axis]
        for j in range(1, 4):
            target = (other + j) % 4
            send_codes(lambda i, target=target: part[axis, target, i], 6, p2s.at[axis, g, j - 1])
            p2(axis, g, j).start()
        for i in range(6):
            keep2[g, i // 3, axis * 3 + i % 3] = part[axis, other, i]

    def p3(k):
        return remote(p3s.at[k], p3r.at[k], p3_s.at[k], p3_r.at[k], dev(dz=offset(k)))

    def third_stage(g):
        for axis in range(2):
            units = []
            for j in range(1, 4):
                p2(axis, g, j).wait_recv()
                units.append(unit_of(p2r.at[axis, g, j - 1]))
            for i in range(6):
                total = keep2[g, i // 3, axis * 3 + i % 3]
                for j in range(3):
                    total += decode(p2r.at[axis, g, j], i, units[j])
                keep2[g, i // 3, axis * 3 + i % 3] = total
        for zi in range(2):
            k = 2 * g + zi

            def out(zi=zi, k=k):
                send_codes(lambda i: keep2[g, zi, i], 6, p3s.at[k])
                p3(k).start()

            if zi == 0:
                out()
            else:
                pl.when(g < GROUPS - 1)(out)

    def c_tile(k, half, i):
        return s_buf[k, half, rows_of(i // 2, 96 + 16 * (i % 2)), :]

    def c1(d, s):
        whole = c1s.at[d, s - 1], c1r.at[d, s - 1]
        if s == 4:
            whole = tuple(ref.at[pl.ds(0, 17)] for ref in whole)
        return remote(*whole, c1_s.at[d, s - 1], c1_r.at[d, s - 1], dev(dz=1 if d == 0 else 7))

    def z_index(d, distance):
        return 0 if distance == 4 else 7 - 2 * distance + d

    def z_hop(d, s):
        if s > 1:
            c1(d, s - 1).wait_recv()
            message = c1r.at[d, s - 2]
            unit = unit_of(message)

        def load(i):
            if i < 16:
                value = c_tile(z_index(d, 5 - s), d, i)
            else:
                value = c_tile(z_index(d, 4 - s), 1 - d, i - 16)
            return value + decode(message, i, unit) if s > 1 else value

        send_codes(load, 32 if s < 4 else 16, c1s.at[d, s - 1])
        c1(d, s).start()

    def c2(j):
        return remote(c2s.at[j - 1], c2r.at[j - 1], c2_s.at[j - 1], c2_r.at[j - 1], dev(dx=j))

    def c3(j):
        return remote(c3s.at[j - 1], c3r.at[j - 1], c3_s.at[j - 1], c3_r.at[j - 1], dev(dy=j))

    def c_second():
        for d in range(2):
            c1(d, 4).wait_recv()
        for half in range(2):
            far, near = c1r.at[half, 3], c1r.at[1 - half, 2]
            far_unit, near_unit = unit_of(far), unit_of(near)
            for i in range(16):
                block, t = i // 2, i % 2
                total = c_tile(7, half, i) + decode(far, i, far_unit) + decode(near, i + 16, near_unit)
                rc[block % 4, half * 2 + block // 4, t] = total
        for j in range(1, 4):
            target = (x + j) % 4
            send_codes(lambda i, target=target: rc[target, i // 2, i % 2], 8, c2s.at[j - 1])
            c2(j).start()

    def c_third():
        units = []
        for j in range(1, 4):
            c2(j).wait_recv()
            units.append(unit_of(c2r.at[j - 1]))
        for i in range(8):
            total = rc[x, i // 2, i % 2]
            for j in range(3):
                total += decode(c2r.at[j], i, units[j])
            kc[i // 2, i % 2] = total
        for j in range(1, 4):
            target = (y + j) % 4
            send_codes(lambda i, target=target: kc[target, i], 2, c3s.at[j - 1])
            c3(j).start()

    def c_last():
        units = []
        for j in range(1, 4):
            c3(j).wait_recv()
            units.append(unit_of(c3r.at[j - 1]))
        for i in range(2):
            total = kc[y, i]
            for j in range(3):
                total += decode(c3r.at[j], i, units[j])
            grad[96 + 16 * i : 112 + 16 * i, :] = total

    for j in range(4):
        h_remote(j).wait_recv()

    def multiply(k, carry):
        for half in range(2):
            g_local(k, half).wait()
            g_remote(k, half).wait_recv()
        product = jnp.dot(ht[...], gb[k], preferred_element_type=F32)
        s_buf[k, 0] = product[:, :BLK]
        s_buf[k, 1] = product[:, BLK:]
        return carry

    def round_of(it, carry):
        @pl.when(it < GROUPS)
        def _():
            lax.fori_loop(2 * it, 2 * it + 2, multiply, 0)
            for axis in range(2):
                first_hop(axis, it)

        for s in range(1, 5):
            pl.when(it == s - 1)(functools.partial(z_hop, 0, s))
            pl.when(it == s)(functools.partial(z_hop, 1, s))

        @pl.when((it >= 1) & (it < GROUPS + 1))
        def _():
            for axis in range(2):
                second_hop(axis, it - 1)

        @pl.when((it >= 2) & (it < GROUPS + 2))
        def _():
            for axis in range(2):
                second_stage(axis, it - 2)

        pl.when(it == GROUPS + 1)(c_second)

        @pl.when(it >= 3)
        def _():
            third_stage(it - 3)

        return carry

    lax.fori_loop(0, GROUPS + 3, round_of, 0)
    c_third()
    units = []
    for k in range(7):
        p3(k).wait_recv()
        units.append(unit_of(p3r.at[k]))
    for i in range(6):
        total = keep2[GROUPS - 1, 1, i]
        for k in range(7):
            total += decode(p3r.at[k], i, units[k])
        grad[16 * i : 16 * i + 16, :] = total
    c_last()

    gradient = grad[...]
    new_first = 0.9 * first_ref[...] + 0.1 * gradient
    new_second = 0.95 * second_ref[...] + 0.05 * gradient * gradient
    update = (
        new_first
        / (1.0 - 0.9**ADAM_STEP)
        / (jnp.sqrt(new_second / (1.0 - 0.95**ADAM_STEP)) + 1e-08)
    )
    master = master_ref[...]
    new_master = master - 0.02 * (update + 0.1 * master)
    new_master_ref[...] = new_master
    new_first_ref[...] = new_first
    new_second_ref[...] = new_second

    def w_at(dz=0, dy=0, dc=0):
        block = dev(dz=dz, dy=dy, dc=dc)[0]
        return w_buf.at[:, pl.ds(pl.multiple_of(block * BLK, BLK), BLK)]

    def w_z(j):
        return remote(w_at(), w_at(), wz_s.at[j - 1], wz_r.at[j - 1], dev(dz=j))

    def w_z_got(j):
        return remote(w_at(dz=-j), w_at(dz=-j), wz_s.at[j - 1], wz_r.at[j - 1], dev(dz=j))

    def w_y(j, dy=0):
        return remote(w_at(dz=-j, dy=dy), w_at(dz=-j, dy=dy), wy_s.at[j], wy_r.at[j], dev(dy=2))

    def w_c(j, dy, dc=0):
        at = w_at(dz=-j, dy=dy, dc=dc)
        return remote(at, at, wc_s.at[dy // 2, j], wc_r.at[dy // 2, j], dev(dc=1))

    w_at()[...] = new_master.astype(BF16)
    for j in (4, 3, 5, 2, 6, 1, 7):
        w_z(j).start()
    w_y(0).start()
    w_c(0, 0).start()
    for j in (1, 7, 2, 6, 3, 5, 4):
        w_z_got(j).wait_recv()
        w_y(j).start()
        w_c(j, 0).start()
    for j in (0, 1, 7, 2, 6, 3, 5, 4):
        w_y(j, dy=2).wait_recv()
        w_c(j, 2).start()
    for j in range(8):
        for dy in (0, 2):
            w_c(j, dy, dc=1).wait_recv()
    out = pltpu.make_async_copy(w_buf, w_hbm, wo_sem)
    out.start()

    for j in range(4):
        h_remote(j).wait_send()
    for k in range(8):
        for half in range(2):
            g_remote(k, half).wait_send()
    for axis in range(2):
        for g in range(GROUPS):
            for d in range(2):
                one(axis, g, d).wait_send()
                two(axis, g, d).wait_send()
            for j in range(1, 4):
                p2(axis, g, j).wait_send()
    for k in range(7):
        p3(k).wait_send()
    for d in range(2):
        for s in range(1, 5):
            c1(d, s).wait_send()
    for j in range(1, 4):
        c2(j).wait_send()
        c3(j).wait_send()
    for j in range(1, 8):
        w_z(j).wait_send()
    for j in range(8):
        w_y(j).wait_send()
        for dy in (0, 2):
            w_c(j, dy).wait_send()
    out.wait()


def body(hidden_acts, out_grad, live_counts, master, first, second):
    vmem, smem, anywhere = (pl.BlockSpec(memory_space=m) for m in (pltpu.VMEM, pltpu.SMEM, pl.ANY))
    dma = pltpu.SemaphoreType.DMA

    def tiles(*shape, kind=I16):
        return pltpu.VMEM((*shape, 16, BLK), kind)

    block = jax.ShapeDtypeStruct((BLK, BLK), F32)
    return pl.pallas_call(
        kernel,
        out_shape=(block, block, block, jax.ShapeDtypeStruct((BLK, D), BF16)),
        in_specs=[anywhere, anywhere, smem, vmem, vmem, vmem],
        out_specs=(vmem, vmem, vmem, anywhere),
        scratch_shapes=[
            pltpu.VMEM((TOK, FFW), BF16),
            pltpu.VMEM((FFW, 2 * TOK), BF16),
            pltpu.VMEM((8, 2 * TOK, 256), BF16),
            pltpu.VMEM((8, 2, FFW, BLK), F32),
            tiles(4, 2, 25), tiles(4, 2, 25), tiles(4, 2, 25), tiles(4, 2, 25),
            tiles(4, 2, 13), tiles(4, 2, 13), tiles(4, 2, 13), tiles(4, 2, 13),
            tiles(2, 4, 6, kind=F32), tiles(4, 2, 6, kind=F32),
            tiles(2, 4, 3, 7), tiles(2, 4, 3, 7),
            tiles(7, 7), tiles(7, 7),
            tiles(2, 4, 33), tiles(2, 4, 33), tiles(4, 4, 2, kind=F32),
            tiles(3, 9), tiles(3, 9), tiles(4, 2, kind=F32),
            tiles(3, 3), tiles(3, 3),
            pltpu.VMEM((BLK, BLK), F32),
            pltpu.VMEM((BLK, D), BF16),
            dma((4,)), dma((8, 2)), dma((8, 2)), dma((8, 2)), dma((4,)), dma((4,)),
            dma((2, 4, 2)), dma((2, 4, 2)), dma((2, 4, 2)), dma((2, 4, 2)),
            dma((2, 4, 3)), dma((2, 4, 3)), dma((7,)), dma((7,)),
            dma((2, 4)), dma((2, 4)), dma((3,)), dma((3,)), dma((3,)), dma((3,)),
            dma((7,)), dma((7,)), dma((8,)), dma((8,)), dma((2, 8)), dma((2, 8)), dma(()),
        ],
        compiler_params=pltpu.CompilerParams(
            collective_id=0, has_side_effects=True, vmem_limit_bytes=60 * 1024 * 1024
        ),
        cost_estimate=pl.CostEstimate(
            flops=2 * TOK * FFW * D, bytes_accessed=12 * 1024 * 1024, transcendentals=0
        ),
        name="grad_update",
    )(hidden_acts, out_grad, live_counts, master, first, second)


def solution(mesh):
    in_specs = (
        P(("node", "local"), None),
        P(("node", "local"), None),
        P("node", "local"),
        P("local", "node"),
        P("local", "node"),
        P("local", "node"),
    )
    out_specs = (P("local", "node"), P("local", "node"), P("local", "node"), P("local", None))
    return jax.shard_map(body, mesh=mesh, in_specs=in_specs, out_specs=out_specs, check_vma=False)
```

time: 378 us -> 78.3 us (0.21)
  waiting for transfers between devices: 341 us -> 0 us
  Pallas kernels: 0 us -> 70 us
  matrix products: 14.8 us -> 0 us
  between operations: 14.6 us -> 1.29 us
    reduce_scatter x2 -> x0, waiting for transfers between devices: 260 us -> none  [the longest x1 220 us: body(): lax.psum_scatter(lax.dot_general(masked, hidden_acts, (((0,), (0,)), ((),...]
    all_gather x1 -> x0, waiting for transfers between devices: 81.5 us -> none  [body(): lax.all_gather(new_master.astype(jnp.bfloat16), 'node', axis=1, tiled=True)]
    pallas_call x0 -> x1, Pallas kernels: none -> 70 us  [body(): pl.pallas_call(kernel, out_shape=(block, block, block, jax.ShapeDtypeStru...]
    dot_general x1 -> x0, matrix products: 14.8 us -> none  [body(): lax.dot_general(masked, hidden_acts, (((0,), (0,)), ((), ())), preferred_...]
  transfers between devices with their start and end apart: 3 -> 0, of which waited for: 3 -> 0; matrix products, arithmetic and copies ran while one was open for 1% -> 0% of each run, Pallas kernels for 0% -> 0%
where the time goes in v1:
time: 78.3 us; the launch traced here: 78 us
  Pallas kernels  70 us (89%)
  local copies, waits for them, and re-layouts  6.7 us (9%)
  between operations  1.29 us (2%)
    pallas_call x1, Pallas kernels, body(): pl.pallas_call(kernel, out_shape=(block, block, block, jax.ShapeDtypeStru...  70 us
    unnamed x4, local copies, waits for them, and re-layouts  6.7 us

profile of v1, /device:TPU:1, one launch (start us, length us, event | category | flops | bytes accessed | tf_op | source)
XLA Modules:
  0.0 78.0 jit_solution(14777488435794573271)
XLA Ops:
  1.3 70.0 %grad_update.1 = (f32[128,128]{1,0:T(8,128)}, f32[128,128]{1,0:T(8,128)}, f32[128,128]{1,0:T(8,128)}, bf16[128,4096]{1,0:T(8,128)(2,1)}) custom-call(bf16[1024,1024]{1,0:T(8,128)(2,1)} %h_hbm.1, bf16[1024,4096]{1,0:T(8,128)(2,1)} %g_hbm.1, s32[1,1]{1,0:T(1,128)S(6)} %copy.14.live_ref, f32[128,128]{1,0:T(8,128)} %master_ref.1, f32[128,128]{1,0:T(8,128)} %first_ref.1, ...), custom_call_target="tpu_custom_call" | custom-call | flops 8589934592 | bytes 12582912 | tf_op jit(solution)/shard_map/grad_update/pallas_call | solution.py:435
  71.3 1.5 %copy.15 = f32[128,128]{1,0:T(8,128)} copy(f32[128,128]{1,0:T(8,128)} %get-tuple-element.8) | data formatting | bytes 131072
  72.8 1.5 %copy.16 = f32[128,128]{1,0:T(8,128)} copy(f32[128,128]{1,0:T(8,128)} %get-tuple-element.9) | data formatting | bytes 131072
  74.3 1.5 %copy.17 = f32[128,128]{1,0:T(8,128)} copy(f32[128,128]{1,0:T(8,128)} %get-tuple-element.10) | data formatting | bytes 131072
  75.7 2.3 %copy.18 = bf16[128,4096]{1,0:T(8,128)(2,1)} copy(bf16[128,4096]{1,0:T(8,128)(2,1)} %get-tuple-element.11) | data formatting | bytes 2097152

commit v2 on v0

v2 whole, which is shorter than its diff:
```python
import functools

import jax
import jax.numpy as jnp
from jax import lax
from jax.experimental import pallas as pl
from jax.experimental.pallas import tpu as pltpu
from jax.sharding import PartitionSpec as P

ADAM_STEP = 10
MESH = pl.DeviceIdType.MESH
F32, BF16, I16, I32 = jnp.float32, jnp.bfloat16, jnp.int16, jnp.int32
NX, NY, NZ = 4, 4, 8
TOK, FFW, D = 1024, 1024, 4096
BLK = 128
GROUPS = 4
TOP = 32000.0
Z_AT = ((2, 3), (5, 6), (8, 8), (10, 10))


def send_codes(load, count, out):
    peak = functools.reduce(jnp.maximum, [jnp.abs(load(i)) for i in range(count)])
    power = jnp.ceil(jnp.log2(jnp.maximum(peak, 1e-30)) * 64.0)
    scale = jnp.exp2(power * (-1.0 / 64.0)) * TOP
    out[0] = power.astype(I32).astype(I16)
    for i in range(count):
        out[i + 1] = jnp.round(load(i) * scale).astype(I32).astype(I16)


def unit_of(message):
    return jnp.exp2(message[0].astype(I32).astype(F32) * (1.0 / 64.0)) * (1.0 / TOP)


def decode(message, i, unit):
    return message[i + 1].astype(I32).astype(F32) * unit


def adamw(grad, master, first, second):
    new_first = 0.9 * first + 0.1 * grad
    new_second = 0.95 * second + 0.05 * grad * grad
    update = (
        new_first
        / (1.0 - 0.9**ADAM_STEP)
        / (jnp.sqrt(new_second / (1.0 - 0.95**ADAM_STEP)) + 1e-08)
    )
    return master - 0.02 * (update + 0.1 * master), new_first, new_second


def kernel(
    h_hbm, g_hbm, live_ref, master_ref, first_ref, second_ref,
    new_master_ref, new_first_ref, new_second_ref, w_ref,
    h_buf, ht, gb, xs, xr, s_buf, m1s, m1r, m2s, m2r, part, keep2, p2s, p2r, p3s, p3r,
    c1s, c1r, c4s, c4r, rc, c2s, c2r, kc, c3s, c3r, grad, w_buf,
    h_sem, gl_sem, xs_sem, xr_sem, one_s, one_r, two_s, two_r, p2_s, p2_r, p3_s, p3_r,
    c1_s, c1_r, c4_s, c2_s, c2_r, c3_s, c3_r, wz_s, wz_r, wy_s, wy_r, wc_s, wc_r,
):
    node, local = lax.axis_index("node"), lax.axis_index("local")
    core, z, yh = node % 2, (node // 2) % NZ, node // 16
    x, yl = local % 4, local // 4
    y = yh * 2 + yl

    def dev(dx=0, dy=0, dz=0, dc=0):
        tx, ty, tz, tc = (x + dx) % NX, (y + dy) % NY, (z + dz) % NZ, (core + dc) % 2
        return ((ty // 2) * 16 + tz * 2 + tc, (ty % 2) * 4 + tx)

    def remote(src, dst, send, recv, to):
        return pltpu.make_async_remote_copy(
            src_ref=src, dst_ref=dst, send_sem=send, recv_sem=recv, device_id=to, device_id_type=MESH
        )

    def offset(k):
        return 4 + k // 2 - (k % 2) * (1 + 2 * (k // 2))

    def cols(k, half, c):
        block = half * 16 + ((z + offset(k)) % NZ) * 2 + c
        return pl.ds(pl.multiple_of(block * BLK, BLK), BLK)

    def g_local(k, whose, half):
        return pltpu.make_async_copy(
            g_hbm.at[:, cols(k, half, (core + whose) % 2)],
            gb.at[k, :, pl.ds((2 * whose + half) * BLK, BLK)],
            gl_sem.at[k],
        )

    def swap(k):
        return remote(xs.at[k], xr.at[k], xs_sem, xr_sem.at[k], dev(dc=1))

    def wait_for(ref, sem):
        pltpu.make_async_copy(ref, ref, sem).wait()

    def h_load(j):
        return pltpu.make_async_copy(h_hbm.at[:, pl.ds(j * 256, 256)], h_buf.at[:, pl.ds(j * 256, 256)], h_sem.at[j])

    barrier = pltpu.get_barrier_semaphore()
    partners = [dict(dx=1), dict(dx=2), dict(dx=3), dict(dy=1), dict(dy=2), dict(dy=3), dict(dc=1)]
    partners += [dict(dz=i) for i in range(1, NZ)]
    for partner in partners:
        pl.semaphore_signal(barrier, inc=1, device_id=dev(**partner), device_id_type=MESH)
    for j in range(4):
        h_load(j).start()
    for k in range(8):
        for whose in range(2):
            for half in range(2):
                g_local(k, whose, half).start()

    live = live_ref[0, 0]

    def turn(j):
        h_load(j).wait()
        alive = lax.broadcasted_iota(I32, (TOK, 256), 0) < live
        block = jnp.where(alive, h_buf[:, pl.ds(j * 256, 256)].astype(F32), 0.0)
        ht[pl.ds(j * 256, 256), :] = block.T.astype(BF16)

    for j in range(4):
        turn(j)
    pl.semaphore_wait(barrier, len(partners))

    def rows_of(block, start, count=16):
        return pl.ds(pl.multiple_of(block * BLK + start, 16), count)

    def a_tile(k, tx, half, i):
        return s_buf[k, half, rows_of((i // 3) * 4 + tx, 16 * (i % 3)), :]

    def b_tile(k, ty, half, i):
        return s_buf[k, ty // 2, rows_of((ty % 2) * 4 + 2 * half + i // 3, 48 + 16 * (i % 3)), :]

    def hop(stage, axis, k, d):
        src, dst, send, recv = ((m1s, m1r, one_s, one_r.at[k]), (m2s, m2r, two_s, two_r.at[k // 2]))[stage]
        step = 1 if d == 0 else 3
        to = dev(dx=step) if axis == 0 else dev(dy=step)
        return remote(src.at[k, axis, d], dst.at[k, axis, d], send, recv, to)

    tiles = (a_tile, b_tile)
    here = (x, y)

    def first_hop(k):
        for axis in range(2):
            tile, me = tiles[axis], here[axis]
            for d in range(2):
                near = (me + (1 if d == 0 else 3)) % 4
                far = (me + 2) % 4

                def load(i, d=d, near=near, far=far, tile=tile):
                    return tile(k, far, d, i) if i < 6 else tile(k, near, 1 - d, i - 6)

                send_codes(load, 12, m1s.at[k, axis, d])
                hop(0, axis, k, d).start()

    def second_hop(k):
        wait_for(m1r.at[k], one_r.at[k])
        for axis in range(2):
            tile, me = tiles[axis], here[axis]
            for d in range(2):
                near = (me + (1 if d == 0 else 3)) % 4
                message = m1r.at[k, axis, d]
                unit = unit_of(message)

                def load(i, d=d, near=near, message=message, unit=unit, tile=tile):
                    return tile(k, near, d, i) + decode(message, i, unit)

                send_codes(load, 6, m2s.at[k, axis, d])
                hop(1, axis, k, d).start()

    def p2(axis, g, j):
        to = dev(dy=j) if axis == 0 else dev(dx=j)
        return remote(p2s.at[g, axis, j - 1], p2r.at[g, axis, j - 1], p2_s, p2_r.at[g], to)

    def second_stage(g):
        wait_for(m2r.at[pl.ds(2 * g, 2)], two_r.at[g])
        for axis in range(2):
            tile, me = tiles[axis], here[axis]
            for zi in range(2):
                k = 2 * g + zi
                for half in range(2):
                    far, near = m2r.at[k, axis, half], m1r.at[k, axis, 1 - half]
                    far_unit, near_unit = unit_of(far), unit_of(near)
                    for i in range(6):
                        total = tile(k, me, half, i) + decode(far, i, far_unit) + decode(near, i + 6, near_unit)
                        part[axis, 2 * half + i // 3, zi * 3 + i % 3] = total
            other = here[1 - axis]
            for j in range(1, 4):
                target = (other + j) % 4
                send_codes(lambda i, axis=axis, target=target: part[axis, target, i], 6, p2s.at[g, axis, j - 1])
                p2(axis, g, j).start()
            for i in range(6):
                keep2[g, i // 3, axis * 3 + i % 3] = part[axis, other, i]

    def p3(k):
        return remote(p3s.at[k], p3r.at[k], p3_s, p3_r, dev(dz=offset(k)))

    def third_stage(g):
        wait_for(p2r.at[g], p2_r.at[g])
        for axis in range(2):
            units = [unit_of(p2r.at[g, axis, j]) for j in range(3)]
            for i in range(6):
                total = keep2[g, i // 3, axis * 3 + i % 3]
                for j in range(3):
                    total += decode(p2r.at[g, axis, j], i, units[j])
                keep2[g, i // 3, axis * 3 + i % 3] = total
        for zi in range(2):
            k = 2 * g + zi

            def out(zi=zi, k=k):
                send_codes(lambda i: keep2[g, zi, i], 6, p3s.at[k])
                p3(k).start()

            if zi == 0:
                out()
            else:
                pl.when(g < GROUPS - 1)(out)

    def c_tile(k, half, i):
        return s_buf[k, half, rows_of(i // 2, 96 + 16 * (i % 2)), :]

    def c1(d, s):
        src, dst, send = (c1s.at[d, s - 1], c1r.at[d, s - 1], c1_s) if s < 4 else (c4s.at[d], c4r.at[d], c4_s)
        return remote(src, dst, send, c1_r.at[d, s - 1], dev(dz=1 if d == 0 else 7))

    def z_index(d, distance):
        return 0 if distance == 4 else 7 - 2 * distance + d

    def z_hop(d, s):
        if s > 1:
            c1(d, s - 1).wait_recv()
            message = c1r.at[d, s - 2]
            unit = unit_of(message)

        def load(i):
            if i < 16:
                value = c_tile(z_index(d, 5 - s), d, i)
            else:
                value = c_tile(z_index(d, 4 - s), 1 - d, i - 16)
            return value + decode(message, i, unit) if s > 1 else value

        send_codes(load, 32 if s < 4 else 16, c1s.at[d, s - 1] if s < 4 else c4s.at[d])
        c1(d, s).start()

    def c2(j):
        return remote(c2s.at[j - 1], c2r.at[j - 1], c2_s, c2_r, dev(dx=j))

    def c3(j):
        return remote(c3s.at[j - 1], c3r.at[j - 1], c3_s, c3_r, dev(dy=j))

    def c_second():
        for d in range(2):
            c1(d, 4).wait_recv()
        for half in range(2):
            far, near = c4r.at[half], c1r.at[1 - half, 2]
            far_unit, near_unit = unit_of(far), unit_of(near)
            for i in range(16):
                block, t = i // 2, i % 2
                total = c_tile(7, half, i) + decode(far, i, far_unit) + decode(near, i + 16, near_unit)
                rc[block % 4, half * 2 + block // 4, t] = total
        for j in range(1, 4):
            target = (x + j) % 4
            send_codes(lambda i, target=target: rc[target, i // 2, i % 2], 8, c2s.at[j - 1])
            c2(j).start()

    def c_third():
        wait_for(c2r, c2_r)
        units = [unit_of(c2r.at[j]) for j in range(3)]
        for i in range(8):
            total = rc[x, i // 2, i % 2]
            for j in range(3):
                total += decode(c2r.at[j], i, units[j])
            kc[i // 2, i % 2] = total
        for j in range(1, 4):
            target = (y + j) % 4
            send_codes(lambda i, target=target: kc[target, i], 2, c3s.at[j - 1])
            c3(j).start()

    def c_last():
        wait_for(c3r, c3_r)
        units = [unit_of(c3r.at[j]) for j in range(3)]
        for i in range(2):
            total = kc[y, i]
            for j in range(3):
                total += decode(c3r.at[j], i, units[j])
            grad[96 + 16 * i : 112 + 16 * i, :] = total

    def multiply(k):
        wait_for(gb.at[k], gl_sem.at[k])
        product = jnp.dot(ht[...], gb[k], preferred_element_type=F32)
        for half in range(2):
            s_buf[k, half] = product[:, half * BLK : half * BLK + BLK]
            xs[k, half] = product[:, (2 + half) * BLK : (3 + half) * BLK]
        swap(k).start()

    def add_core(k):
        swap(k).wait_recv()

        def add(block, carry):
            rows = rows_of(block, 0, BLK)
            for half in range(2):
                s_buf[k, half, rows, :] += xr[k, half, rows, :]
            return carry

        lax.fori_loop(0, 8, add, 0)

    def round_of(it, carry):
        pl.when(it < 8)(lambda: multiply(it))

        @pl.when((it >= 1) & (it < 9))
        def _():
            add_core(it - 1)
            first_hop(it - 1)

        for s, when in enumerate(Z_AT, 1):
            for d in range(2):
                pl.when(it == when[d])(functools.partial(z_hop, d, s))

        pl.when((it >= 3) & (it < 11))(lambda: second_hop(it - 3))
        pl.when((it >= 6) & (it < 13) & (it % 2 == 0))(lambda: second_stage((it - 6) // 2))
        pl.when(it == 12)(c_second)
        pl.when((it >= 8) & (it % 2 == 0))(lambda: third_stage((it - 8) // 2))
        return carry

    lax.fori_loop(0, 15, round_of, 0)
    c_third()
    wait_for(p3r, p3_r)
    units = [unit_of(p3r.at[k]) for k in range(7)]
    for i in range(6):
        total = keep2[GROUPS - 1, 1, i]
        for k in range(7):
            total += decode(p3r.at[k], i, units[k])
        grad[16 * i : 16 * i + 16, :] = total
    c_last()

    new_master, new_first, new_second = adamw(grad[...], master_ref[...], first_ref[...], second_ref[...])

    def w_at(dz=0, dy=0, dc=0):
        block = dev(dz=dz, dy=dy, dc=dc)[0]
        return w_buf.at[:, pl.ds(pl.multiple_of(block * BLK, BLK), BLK)]

    z_sends = ((0, 1, 0, BLK), (0, 7, 0, BLK), (0, 2, 0, BLK), (0, 6, 0, BLK), (6, 1, 0, BLK), (2, 7, 0, BLK), (6, 2, 0, 64), (2, 6, 64, 64))

    def w_z(i, got=False):
        block, to, start, count = z_sends[i]
        at = w_at(dz=block - to if got else block).at[pl.ds(start, count)]
        return remote(at, at, wz_s, wz_r.at[min(i, 6)], dev(dz=to))

    def w_y(j, dy=0):
        return remote(w_at(dz=-j, dy=dy), w_at(dz=-j, dy=dy), wy_s, wy_r.at[j], dev(dy=2))

    def w_c(j, dy):
        at = w_at(dz=-j, dy=dy)
        return remote(at, at, wc_s, wc_r, dev(dc=1))

    w_at()[...] = new_master.astype(BF16)
    def spread(j):
        w_y(j).start()
        w_c(j, 0).start()

    for i in (2, 3, 0, 1):
        w_z(i).start()
    spread(0)
    new_master_ref[...] = new_master
    new_first_ref[...] = new_first
    new_second_ref[...] = new_second
    w_z(2, got=True).wait_recv()
    w_z(4).start()
    w_z(6).start()
    w_z(3, got=True).wait_recv()
    w_z(5).start()
    w_z(7).start()
    for i, j in ((0, 1), (1, 7)):
        w_z(i, got=True).wait_recv()
        spread(j)
    spread(2)
    spread(6)
    for i, j in ((4, 3), (5, 5)):
        w_z(i, got=True).wait_recv()
        spread(j)
    wait_for(w_at(dz=4), wz_r.at[6])
    spread(4)
    for j in (0, 1, 7, 2, 6, 3, 5, 4):
        w_y(j, dy=2).wait_recv()
        w_c(j, 2).start()
    def blocks(count):
        return w_buf.at[:, pl.ds(0, count * BLK)]

    wait_for(blocks(16), wc_r)
    w_ref[...] = w_buf[...]

    for ref, sem in (
        (xs, xs_sem), (m1s, one_s), (m2s, two_s), (p2s, p2_s), (p3s, p3_s), (c1s, c1_s), (c4s, c4_s), (c2s, c2_s), (c3s, c3_s),
        (blocks(7), wz_s), (blocks(8), wy_s), (blocks(16), wc_s),
    ):
        wait_for(ref, sem)


def body(hidden_acts, out_grad, live_counts, master, first, second):
    vmem, smem, anywhere = (pl.BlockSpec(memory_space=m) for m in (pltpu.VMEM, pltpu.SMEM, pl.ANY))
    dma = pltpu.SemaphoreType.DMA

    def tiles(*shape, kind=I16):
        return pltpu.VMEM((*shape, 16, BLK), kind)

    block = pltpu.VMEM((BLK, BLK), F32)
    return pl.pallas_call(
        kernel,
        out_shape=(block, block, block, pltpu.VMEM((BLK, D), BF16)),
        in_specs=[anywhere, anywhere, smem, vmem, vmem, vmem],
        out_specs=(vmem, vmem, vmem, vmem),
        scratch_shapes=[
            pltpu.VMEM((TOK, FFW), BF16),
            pltpu.VMEM((FFW, TOK), BF16),
            pltpu.VMEM((8, TOK, 4 * BLK), BF16),
            pltpu.VMEM((8, 2, FFW, BLK), F32), pltpu.VMEM((8, 2, FFW, BLK), F32), pltpu.VMEM((8, 2, FFW, BLK), F32),
            tiles(8, 2, 2, 13), tiles(8, 2, 2, 13), tiles(8, 2, 2, 7), tiles(8, 2, 2, 7),
            tiles(2, 4, 6, kind=F32), tiles(4, 2, 6, kind=F32),
            tiles(4, 2, 3, 7), tiles(4, 2, 3, 7), tiles(7, 7), tiles(7, 7),
            tiles(2, 3, 33), tiles(2, 3, 33), tiles(2, 17), tiles(2, 17), tiles(4, 4, 2, kind=F32),
            tiles(3, 9), tiles(3, 9), tiles(4, 2, kind=F32), tiles(3, 3), tiles(3, 3),
            pltpu.VMEM((BLK, BLK), F32),
            pltpu.VMEM((BLK, D), BF16),
            dma((4,)), dma((8,)), dma(()), dma((8,)), dma(()), dma((8,)), dma(()), dma((4,)), dma(()), dma((4,)), dma(()), dma(()),
            dma(()), dma((2, 4)), dma(()), dma(()), dma(()), dma(()), dma(()),
            dma(()), dma((7,)), dma(()), dma((8,)), dma(()), dma(()),
        ],
        compiler_params=pltpu.CompilerParams(
            collective_id=0, has_side_effects=True, vmem_limit_bytes=60 * 1024 * 1024
        ),
        cost_estimate=pl.CostEstimate(
            flops=2 * TOK * FFW * D, bytes_accessed=12 * 1024 * 1024, transcendentals=0
        ),
        name="grad_update",
    )(hidden_acts, out_grad, live_counts, master, first, second)

def solution(mesh):
    in_specs = (
        P(("node", "local"), None),
        P(("node", "local"), None),
        P("node", "local"),
        P("local", "node"),
        P("local", "node"),
        P("local", "node"),
    )
    out_specs = (P("local", "node"), P("local", "node"), P("local", "node"), P("local", None))
    return jax.shard_map(body, mesh=mesh, in_specs=in_specs, out_specs=out_specs, check_vma=False)
```

time: 378 us -> 69.5 us (0.18)
  waiting for transfers between devices: 341 us -> 0 us
  Pallas kernels: 0 us -> 65.2 us
  matrix products: 14.8 us -> 0 us
  between operations: 14.6 us -> 1.29 us
    reduce_scatter x2 -> x0, waiting for transfers between devices: 260 us -> none  [the longest x1 220 us: body(): lax.psum_scatter(lax.dot_general(masked, hidden_acts, (((0,), (0,)), ((),...]
    all_gather x1 -> x0, waiting for transfers between devices: 81.5 us -> none  [body(): lax.all_gather(new_master.astype(jnp.bfloat16), 'node', axis=1, tiled=True)]
    pallas_call x0 -> x1, Pallas kernels: none -> 65.2 us  [body(): pl.pallas_call(kernel, out_shape=(block, block, block, pltpu.VMEM((BLK, D...]
    dot_general x1 -> x0, matrix products: 14.8 us -> none  [body(): lax.dot_general(masked, hidden_acts, (((0,), (0,)), ((), ())), preferred_...]
  transfers between devices with their start and end apart: 3 -> 0, of which waited for: 3 -> 0; matrix products, arithmetic and copies ran while one was open for 1% -> 0% of each run, Pallas kernels for 0% -> 0%
where the time goes in v2:
time: 69.5 us; the launch traced here: 69.4 us
  Pallas kernels  65.2 us (94%)
  local copies, waits for them, and re-layouts  2.86 us (4%)
  between operations  1.29 us (2%)
    pallas_call x1, Pallas kernels, body(): pl.pallas_call(kernel, out_shape=(block, block, block, pltpu.VMEM((BLK, D...  65.2 us
    unnamed x4, local copies, waits for them, and re-layouts  2.86 us

profile of v2, /device:TPU:1, one launch (start us, length us, event | category | flops | bytes accessed | tf_op | source)
XLA Modules:
  0.0 69.4 jit_solution(15156174030623556758)
XLA Ops:
  1.3 65.2 %grad_update.1 = (f32[128,128]{1,0:T(8,128)S(1)}, f32[128,128]{1,0:T(8,128)S(1)}, f32[128,128]{1,0:T(8,128)S(1)}, bf16[128,4096]{1,0:T(8,128)(2,1)S(1)}) custom-call(bf16[1024,1024]{1,0:T(8,128)(2,1)} %h_hbm.1, bf16[1024,4096]{1,0:T(8,128)(2,1)} %g_hbm.1, s32[1,1]{1,0:T(1,128)S(6)} %copy.18.live_ref, f32[128,128]{1,0:T(8,128)} %master_ref.1, ...), custom_call_target="tpu_custom_call" | custom-call | flops 8589934592 | bytes 12582912 | tf_op jit(solution)/shard_map/grad_update/pallas_call | solution.py:400
  66.5 0.6 copy.14
  67.1 0.6 copy.15
  67.8 0.6 copy.16
  68.4 1.0 %copy.17 = bf16[128,4096]{1,0:T(8,128)(2,1)} copy(bf16[128,4096]{1,0:T(8,128)(2,1)S(1)} %get-tuple-element.7) | data formatting | bytes 2097152

commit v3 on v2

--- a/solution.py
+++ b/solution.py
@@ -15,7 +15,9 @@
 BLK = 128
 GROUPS = 4
 TOP = 32000.0
-Z_AT = ((2, 3), (5, 6), (8, 8), (10, 10))
+Z_AT = ((2, 3), (4, 5), (6, 7), (8, 9))
+C_AT = (11, 13)
+LAG = (3, 6, 8)
 
 
 def send_codes(load, count, out):
@@ -46,44 +48,56 @@
     return master - 0.02 * (update + 0.1 * master), new_first, new_second
 
 
+def hand_out(*refs):
+    sources, targets, sem = refs[:4], refs[4:8], refs[8]
+    copies = [pltpu.make_async_copy(a, b, sem.at[i]) for i, (a, b) in enumerate(zip(sources, targets))]
+    for copy in copies:
+        copy.start()
+    for copy in copies:
+        copy.wait()
+
+
 def kernel(
     h_hbm, g_hbm, live_ref, master_ref, first_ref, second_ref,
     new_master_ref, new_first_ref, new_second_ref, w_ref,
     h_buf, ht, gb, xs, xr, s_buf, m1s, m1r, m2s, m2r, part, keep2, p2s, p2r, p3s, p3r,
-    c1s, c1r, c4s, c4r, rc, c2s, c2r, kc, c3s, c3r, grad, w_buf,
+    c1s, c1r, rc, c2s, c2r, kc, c3s, c3r, grad, w_buf,
     h_sem, gl_sem, xs_sem, xr_sem, one_s, one_r, two_s, two_r, p2_s, p2_r, p3_s, p3_r,
-    c1_s, c1_r, c4_s, c2_s, c2_r, c3_s, c3_r, wz_s, wz_r, wy_s, wy_r, wc_s, wc_r,
+    c1_s, c1_r, c2_s, c2_r, c3_s, c3_r, wz_s, wz_r, wy_s, wy_r, wc_s, wc_r,
 ):
     node, local = lax.axis_index("node"), lax.axis_index("local")
-    core, z, yh = node % 2, (node // 2) % NZ, node // 16
-    x, yl = local % 4, local // 4
+    core, z, yh = lax.rem(node, 2), lax.rem(lax.div(node, 2), NZ), lax.div(node, 16)
+    x, yl = lax.rem(local, 4), lax.div(local, 4)
     y = yh * 2 + yl
 
-    def dev(dx=0, dy=0, dz=0, dc=0):
-        tx, ty, tz, tc = (x + dx) % NX, (y + dy) % NY, (z + dz) % NZ, (core + dc) % 2
-        return ((ty // 2) * 16 + tz * 2 + tc, (ty % 2) * 4 + tx)
+    xs_at = [lax.rem(x + i, NX) for i in range(NX)]
+    ys_at = [lax.rem(y + i, NY) for i in range(NY)]
+    zs_at = [lax.rem(z + i, NZ) for i in range(NZ)]
+    to_x = [(node, yl * 4 + at) for at in xs_at]
+    to_y = [(lax.div(at, 2) * 16 + lax.rem(node, 16), lax.rem(at, 2) * 4 + x) for at in ys_at]
+    z_nodes = [[half * 16 + at * 2 + core for at in zs_at] for half in (yh, 1 - yh)]
+    to_z = [(at, local) for at in z_nodes[0]]
+    to_core = (node + 1 - 2 * core, local)
 
     def remote(src, dst, send, recv, to):
         return pltpu.make_async_remote_copy(
             src_ref=src, dst_ref=dst, send_sem=send, recv_sem=recv, device_id=to, device_id_type=MESH
         )
 
-    def offset(k):
-        return 4 + k // 2 - (k % 2) * (1 + 2 * (k // 2))
-
-    def cols(k, half, c):
-        block = half * 16 + ((z + offset(k)) % NZ) * 2 + c
+    def cols(k, half, whose):
+        away = 4 + k // 2 if k % 2 == 0 else 3 - k // 2
+        block = half * 16 + zs_at[away] * 2 + (1 - core if whose else core)
         return pl.ds(pl.multiple_of(block * BLK, BLK), BLK)
 
     def g_local(k, whose, half):
         return pltpu.make_async_copy(
-            g_hbm.at[:, cols(k, half, (core + whose) % 2)],
+            g_hbm.at[:, cols(k, half, whose)],
             gb.at[k, :, pl.ds((2 * whose + half) * BLK, BLK)],
             gl_sem.at[k],
         )
 
     def swap(k):
-        return remote(xs.at[k], xr.at[k], xs_sem, xr_sem.at[k], dev(dc=1))
+        return remote(xs.at[k], xr.at[k], xs_sem, xr_sem.at[k], to_core)
 
     def wait_for(ref, sem):
         pltpu.make_async_copy(ref, ref, sem).wait()
@@ -92,10 +106,9 @@
         return pltpu.make_async_copy(h_hbm.at[:, pl.ds(j * 256, 256)], h_buf.at[:, pl.ds(j * 256, 256)], h_sem.at[j])
 
     barrier = pltpu.get_barrier_semaphore()
-    partners = [dict(dx=1), dict(dx=2), dict(dx=3), dict(dy=1), dict(dy=2), dict(dy=3), dict(dc=1)]
-    partners += [dict(dz=i) for i in range(1, NZ)]
+    partners = [*to_x[1:], *to_y[1:], *to_z[1:], to_core]
     for partner in partners:
-        pl.semaphore_signal(barrier, inc=1, device_id=dev(**partner), device_id_type=MESH)
+        pl.semaphore_signal(barrier, inc=1, device_id=partner, device_id_type=MESH)
     for j in range(4):
         h_load(j).start()
     for k in range(8):
@@ -122,23 +135,21 @@
         return s_buf[k, half, rows_of((i // 3) * 4 + tx, 16 * (i % 3)), :]
 
     def b_tile(k, ty, half, i):
-        return s_buf[k, ty // 2, rows_of((ty % 2) * 4 + 2 * half + i // 3, 48 + 16 * (i % 3)), :]
+        return s_buf[k, lax.div(ty, 2), rows_of(lax.rem(ty, 2) * 4 + 2 * half + i // 3, 48 + 16 * (i % 3)), :]
 
     def hop(stage, axis, k, d):
         src, dst, send, recv = ((m1s, m1r, one_s, one_r.at[k]), (m2s, m2r, two_s, two_r.at[k // 2]))[stage]
-        step = 1 if d == 0 else 3
-        to = dev(dx=step) if axis == 0 else dev(dy=step)
+        to = (to_x, to_y)[axis][1 if d == 0 else 3]
         return remote(src.at[k, axis, d], dst.at[k, axis, d], send, recv, to)
 
     tiles = (a_tile, b_tile)
-    here = (x, y)
+    here = (xs_at, ys_at)
 
     def first_hop(k):
         for axis in range(2):
             tile, me = tiles[axis], here[axis]
             for d in range(2):
-                near = (me + (1 if d == 0 else 3)) % 4
-                far = (me + 2) % 4
+                near, far = me[1 if d == 0 else 3], me[2]
 
                 def load(i, d=d, near=near, far=far, tile=tile):
                     return tile(k, far, d, i) if i < 6 else tile(k, near, 1 - d, i - 6)
@@ -151,7 +162,7 @@
         for axis in range(2):
             tile, me = tiles[axis], here[axis]
             for d in range(2):
-                near = (me + (1 if d == 0 else 3)) % 4
+                near = me[1 if d == 0 else 3]
                 message = m1r.at[k, axis, d]
                 unit = unit_of(message)
 
@@ -162,7 +173,7 @@
                 hop(1, axis, k, d).start()
 
     def p2(axis, g, j):
-        to = dev(dy=j) if axis == 0 else dev(dx=j)
+        to = (to_y, to_x)[axis][j]
         return remote(p2s.at[g, axis, j - 1], p2r.at[g, axis, j - 1], p2_s, p2_r.at[g], to)
 
     def second_stage(g):
@@ -175,18 +186,19 @@
                     far, near = m2r.at[k, axis, half], m1r.at[k, axis, 1 - half]
                     far_unit, near_unit = unit_of(far), unit_of(near)
                     for i in range(6):
-                        total = tile(k, me, half, i) + decode(far, i, far_unit) + decode(near, i + 6, near_unit)
+                        total = tile(k, me[0], half, i) + decode(far, i, far_unit) + decode(near, i + 6, near_unit)
                         part[axis, 2 * half + i // 3, zi * 3 + i % 3] = total
             other = here[1 - axis]
             for j in range(1, 4):
-                target = (other + j) % 4
-                send_codes(lambda i, axis=axis, target=target: part[axis, target, i], 6, p2s.at[g, axis, j - 1])
+                send_codes(lambda i, axis=axis, target=other[j]: part[axis, target, i], 6, p2s.at[g, axis, j - 1])
                 p2(axis, g, j).start()
             for i in range(6):
-                keep2[g, i // 3, axis * 3 + i % 3] = part[axis, other, i]
-
-    def p3(k):
-        return remote(p3s.at[k], p3r.at[k], p3_s, p3_r, dev(dz=offset(k)))
+                keep2[g, i // 3, axis * 3 + i % 3] = part[axis, other[0], i]
+
+    def p3(g, zi):
+        k = 2 * g + zi
+        at = lax.rem(z + (3 - g if zi else 4 + g), NZ)
+        return remote(p3s.at[k], p3r.at[k], p3_s, p3_r, (yh * 16 + at * 2 + core, local))
 
     def third_stage(g):
         wait_for(p2r.at[g], p2_r.at[g])
@@ -198,11 +210,10 @@
                     total += decode(p2r.at[g, axis, j], i, units[j])
                 keep2[g, i // 3, axis * 3 + i % 3] = total
         for zi in range(2):
-            k = 2 * g + zi
-
-            def out(zi=zi, k=k):
-                send_codes(lambda i: keep2[g, zi, i], 6, p3s.at[k])
-                p3(k).start()
+
+            def out(zi=zi):
+                send_codes(lambda i: keep2[g, zi, i], 6, p3s.at[2 * g + zi])
+                p3(g, zi).start()
 
             if zi == 0:
                 out()
@@ -212,47 +223,47 @@
     def c_tile(k, half, i):
         return s_buf[k, half, rows_of(i // 2, 96 + 16 * (i % 2)), :]
 
-    def c1(d, s):
-        src, dst, send = (c1s.at[d, s - 1], c1r.at[d, s - 1], c1_s) if s < 4 else (c4s.at[d], c4r.at[d], c4_s)
-        return remote(src, dst, send, c1_r.at[d, s - 1], dev(dz=1 if d == 0 else 7))
+    def c1(d, s, p):
+        i = s - 1 + 4 * p
+        return remote(c1s.at[i, d], c1r.at[i, d], c1_s, c1_r.at[i, d], to_z[1 if d == 0 else 7])
 
     def z_index(d, distance):
         return 0 if distance == 4 else 7 - 2 * distance + d
 
     def z_hop(d, s):
-        if s > 1:
-            c1(d, s - 1).wait_recv()
-            message = c1r.at[d, s - 2]
-            unit = unit_of(message)
-
-        def load(i):
-            if i < 16:
-                value = c_tile(z_index(d, 5 - s), d, i)
-            else:
-                value = c_tile(z_index(d, 4 - s), 1 - d, i - 16)
-            return value + decode(message, i, unit) if s > 1 else value
-
-        send_codes(load, 32 if s < 4 else 16, c1s.at[d, s - 1] if s < 4 else c4s.at[d])
-        c1(d, s).start()
+        for p in range(2 if s < 4 else 1):
+            k, half = z_index(d, 5 - s - p), d if p == 0 else 1 - d
+            if s > 1:
+                c1(d, s - 1, p).wait_recv()
+                message = c1r.at[s - 2 + 4 * p, d]
+                unit = unit_of(message)
+
+            def load(i):
+                value = c_tile(k, half, i)
+                return value + decode(message, i, unit) if s > 1 else value
+
+            send_codes(load, 16, c1s.at[s - 1 + 4 * p, d])
+            c1(d, s, p).start()
 
     def c2(j):
-        return remote(c2s.at[j - 1], c2r.at[j - 1], c2_s, c2_r, dev(dx=j))
+        return remote(c2s.at[j - 1], c2r.at[j - 1], c2_s, c2_r, to_x[j])
 
     def c3(j):
-        return remote(c3s.at[j - 1], c3r.at[j - 1], c3_s, c3_r, dev(dy=j))
+        return remote(c3s.at[j - 1], c3r.at[j - 1], c3_s, c3_r, to_y[j])
 
     def c_second():
         for d in range(2):
-            c1(d, 4).wait_recv()
+            c1(d, 4, 0).wait_recv()
+            c1(d, 3, 1).wait_recv()
         for half in range(2):
-            far, near = c4r.at[half], c1r.at[1 - half, 2]
+            far, near = c1r.at[3, half], c1r.at[6, 1 - half]
             far_unit, near_unit = unit_of(far), unit_of(near)
             for i in range(16):
                 block, t = i // 2, i % 2
-                total = c_tile(7, half, i) + decode(far, i, far_unit) + decode(near, i + 16, near_unit)
+                total = c_tile(7, half, i) + decode(far, i, far_unit) + decode(near, i, near_unit)
                 rc[block % 4, half * 2 + block // 4, t] = total
         for j in range(1, 4):
-            target = (x + j) % 4
+            target = xs_at[j]
             send_codes(lambda i, target=target: rc[target, i // 2, i % 2], 8, c2s.at[j - 1])
             c2(j).start()
 
@@ -265,7 +276,7 @@
                 total += decode(c2r.at[j], i, units[j])
             kc[i // 2, i % 2] = total
         for j in range(1, 4):
-            target = (y + j) % 4
+            target = ys_at[j]
             send_codes(lambda i, target=target: kc[target, i], 2, c3s.at[j - 1])
             c3(j).start()
 
@@ -309,14 +320,14 @@
             for d in range(2):
                 pl.when(it == when[d])(functools.partial(z_hop, d, s))
 
-        pl.when((it >= 3) & (it < 11))(lambda: second_hop(it - 3))
-        pl.when((it >= 6) & (it < 13) & (it % 2 == 0))(lambda: second_stage((it - 6) // 2))
-        pl.when(it == 12)(c_second)
-        pl.when((it >= 8) & (it % 2 == 0))(lambda: third_stage((it - 8) // 2))
+        pl.when((it >= LAG[0]) & (it < LAG[0] + 8))(lambda: second_hop(it - LAG[0]))
+        pl.when((it >= LAG[1]) & (it < LAG[1] + 7) & ((it - LAG[1]) % 2 == 0))(lambda: second_stage((it - LAG[1]) // 2))
+        pl.when(it == C_AT[0])(c_second)
+        pl.when(it == C_AT[1])(c_third)
+        pl.when((it >= LAG[2]) & ((it - LAG[2]) % 2 == 0))(lambda: third_stage((it - LAG[2]) // 2))
         return carry
 
-    lax.fori_loop(0, 15, round_of, 0)
-    c_third()
+    lax.fori_loop(0, LAG[2] + 7, round_of, 0)
     wait_for(p3r, p3_r)
     units = [unit_of(p3r.at[k]) for k in range(7)]
     for i in range(6):
@@ -328,25 +339,32 @@
 
     new_master, new_first, new_second = adamw(grad[...], master_ref[...], first_ref[...], second_ref[...])
 
-    def w_at(dz=0, dy=0, dc=0):
-        block = dev(dz=dz, dy=dy, dc=dc)[0]
-        return w_buf.at[:, pl.ds(pl.multiple_of(block * BLK, BLK), BLK)]
+    def w_at(dz=0, other=0):
+        return w_buf.at[:, pl.ds(pl.multiple_of(z_nodes[other][dz] * BLK, BLK), BLK)]
 
     z_sends = ((0, 1, 0, BLK), (0, 7, 0, BLK), (0, 2, 0, BLK), (0, 6, 0, BLK), (6, 1, 0, BLK), (2, 7, 0, BLK), (6, 2, 0, 64), (2, 6, 64, 64))
 
-    def w_z(i, got=False):
+    def w_z(i):
         block, to, start, count = z_sends[i]
-        at = w_at(dz=block - to if got else block).at[pl.ds(start, count)]
-        return remote(at, at, wz_s, wz_r.at[min(i, 6)], dev(dz=to))
-
-    def w_y(j, dy=0):
-        return remote(w_at(dz=-j, dy=dy), w_at(dz=-j, dy=dy), wy_s, wy_r.at[j], dev(dy=2))
-
-    def w_c(j, dy):
-        at = w_at(dz=-j, dy=dy)
-        return remote(at, at, wc_s, wc_r, dev(dc=1))
+        at = w_at(block).at[pl.ds(start, count)]
+        return remote(at, at, wz_s, wz_r.at[min(i, 6)], to_z[to])
+
+    def blocks(count):
+        return w_buf.at[:, pl.ds(0, count * BLK)]
+
+    def w_z_got(i):
+        wait_for(blocks(1), wz_r.at[i])
+
+    def w_y(j):
+        at = w_at(-j % NZ)
+        return remote(at, at, wy_s, wy_r.at[j], to_y[2])
+
+    def w_c(j, other):
+        at = w_at(-j % NZ, other)
+        return remote(at, at, wc_s, wc_r, to_core)
 
     w_at()[...] = new_master.astype(BF16)
+
     def spread(j):
         w_y(j).start()
         w_c(j, 0).start()
@@ -357,33 +375,28 @@
     new_master_ref[...] = new_master
     new_first_ref[...] = new_first
     new_second_ref[...] = new_second
-    w_z(2, got=True).wait_recv()
+    w_z_got(2)
     w_z(4).start()
     w_z(6).start()
-    w_z(3, got=True).wait_recv()
+    w_z_got(3)
     w_z(5).start()
     w_z(7).start()
     for i, j in ((0, 1), (1, 7)):
-        w_z(i, got=True).wait_recv()
+        w_z_got(i)
         spread(j)
     spread(2)
     spread(6)
-    for i, j in ((4, 3), (5, 5)):
-        w_z(i, got=True).wait_recv()
+    for i, j in ((4, 3), (5, 5), (6, 4)):
+        w_z_got(i)
         spread(j)
-    wait_for(w_at(dz=4), wz_r.at[6])
-    spread(4)
     for j in (0, 1, 7, 2, 6, 3, 5, 4):
-        w_y(j, dy=2).wait_recv()
-        w_c(j, 2).start()
-    def blocks(count):
-        return w_buf.at[:, pl.ds(0, count * BLK)]
-
+        wait_for(blocks(1), wy_r.at[j])
+        w_c(j, 1).start()
     wait_for(blocks(16), wc_r)
     w_ref[...] = w_buf[...]
 
     for ref, sem in (
-        (xs, xs_sem), (m1s, one_s), (m2s, two_s), (p2s, p2_s), (p3s, p3_s), (c1s, c1_s), (c4s, c4_s), (c2s, c2_s), (c3s, c3_s),
+        (xs, xs_sem), (m1s, one_s), (m2s, two_s), (p2s, p2_s), (p3s, p3_s), (c1s, c1_s), (c2s, c2_s), (c3s, c3_s),
         (blocks(7), wz_s), (blocks(8), wy_s), (blocks(16), wc_s),
     ):
         wait_for(ref, sem)
@@ -397,7 +410,7 @@
         return pltpu.VMEM((*shape, 16, BLK), kind)
 
     block = pltpu.VMEM((BLK, BLK), F32)
-    return pl.pallas_call(
+    results = pl.pallas_call(
         kernel,
         out_shape=(block, block, block, pltpu.VMEM((BLK, D), BF16)),
         in_specs=[anywhere, anywhere, smem, vmem, vmem, vmem],
@@ -410,12 +423,12 @@
             tiles(8, 2, 2, 13), tiles(8, 2, 2, 13), tiles(8, 2, 2, 7), tiles(8, 2, 2, 7),
             tiles(2, 4, 6, kind=F32), tiles(4, 2, 6, kind=F32),
             tiles(4, 2, 3, 7), tiles(4, 2, 3, 7), tiles(7, 7), tiles(7, 7),
-            tiles(2, 3, 33), tiles(2, 3, 33), tiles(2, 17), tiles(2, 17), tiles(4, 4, 2, kind=F32),
+            tiles(7, 2, 17), tiles(7, 2, 17), tiles(4, 4, 2, kind=F32),
             tiles(3, 9), tiles(3, 9), tiles(4, 2, kind=F32), tiles(3, 3), tiles(3, 3),
             pltpu.VMEM((BLK, BLK), F32),
             pltpu.VMEM((BLK, D), BF16),
             dma((4,)), dma((8,)), dma(()), dma((8,)), dma(()), dma((8,)), dma(()), dma((4,)), dma(()), dma((4,)), dma(()), dma(()),
-            dma(()), dma((2, 4)), dma(()), dma(()), dma(()), dma(()), dma(()),
+            dma(()), dma((7, 2)), dma(()), dma(()), dma(()), dma(()),
             dma(()), dma((7,)), dma(()), dma((8,)), dma(()), dma(()),
         ],
         compiler_params=pltpu.CompilerParams(
@@ -426,6 +439,14 @@
         ),
         name="grad_update",
     )(hidden_acts, out_grad, live_counts, master, first, second)
+    return pl.pallas_call(
+        hand_out,
+        out_shape=[jax.ShapeDtypeStruct(r.shape, r.dtype) for r in results],
+        in_specs=[vmem] * 4,
+        out_specs=[anywhere] * 4,
+        scratch_shapes=[dma((4,))],
+        name="hand_out",
+    )(*(pltpu.with_memory_space_constraint(r, pltpu.VMEM) for r in results))
 
 def solution(mesh):
     in_specs = (

time: 69.5 us -> 64.9 us (0.934)
  local copies, waits for them, and re-layouts: 2.86 us -> 0 us
  Pallas kernels: 65.2 us -> 63.5 us
    unnamed x4 -> x0, local copies, waits for them, and re-layouts: 2.86 us -> none
    pallas_call x1, Pallas kernels: 65.2 us -> 62.4 us  [body(): pl.pallas_call(kernel, out_shape=(block, block, block, pltpu.VMEM((BLK, D...]
    pallas_call x0 -> x1, Pallas kernels: none -> 1.07 us  [body(): pl.pallas_call(hand_out, out_shape=[jax.ShapeDtypeStruct(r.shape, r.dtype...]
where the time goes in v3:
time: 64.9 us; the launch traced here: 64.8 us
  Pallas kernels  63.5 us (98%)
  between operations  1.29 us (2%)
    pallas_call x1, Pallas kernels, body(): pl.pallas_call(kernel, out_shape=(block, block, block, pltpu.VMEM((BLK, D...  62.4 us

profile of v3, /device:TPU:1, one launch (start us, length us, event | category | flops | bytes accessed | tf_op | source)
XLA Modules:
  0.0 64.8 jit_solution(18243736682174560565)
XLA Ops:
  1.3 62.4 %grad_update.1 = (f32[128,128]{1,0:T(8,128)S(1)}, f32[128,128]{1,0:T(8,128)S(1)}, f32[128,128]{1,0:T(8,128)S(1)}, bf16[128,4096]{1,0:T(8,128)(2,1)S(1)}) custom-call(bf16[1024,1024]{1,0:T(8,128)(2,1)} %h_hbm.1, bf16[1024,4096]{1,0:T(8,128)(2,1)} %g_hbm.1, s32[1,1]{1,0:T(1,128)S(6)} %copy.10.live_ref, f32[128,128]{1,0:T(8,128)} %master_ref.1, ...), custom_call_target="tpu_custom_call" | custom-call | flops 8589934592 | bytes 12582912 | tf_op jit(solution)/shard_map/grad_update/pallas_call | solution.py:413
  63.7 1.1 %hand_out.1 = (f32[128,128]{1,0:T(8,128)}, f32[128,128]{1,0:T(8,128)}, f32[128,128]{1,0:T(8,128)}, bf16[128,4096]{1,0:T(8,128)(2,1)}) custom-call(f32[128,128]{1,0:T(8,128)S(1)} %get-tuple-element.8.refs_0_, f32[128,128]{1,0:T(8,128)S(1)} %get-tuple-element.9.refs_1_, f32[128,128]{1,0:T(8,128)S(1)} %get-tuple-element.10.refs_2_, ...), custom_call_target="tpu_custom_call" | custom-call | tf_op jit(solution)/shard_map/hand_out/pallas_call | solution.py:442

commit v4 on v3

--- a/solution.py
+++ b/solution.py
@@ -15,9 +15,10 @@
 BLK = 128
 GROUPS = 4
 TOP = 32000.0
-Z_AT = ((2, 3), (4, 5), (6, 7), (8, 9))
+Z_AT = ((2, 3), (5, 6), (7, 8), (9, 9))
 C_AT = (11, 13)
-LAG = (3, 6, 8)
+LAG = (4, 7, 9)
+FAR = (4, 3, 5)
 
 
 def send_codes(load, count, out):
@@ -60,7 +61,7 @@
 def kernel(
     h_hbm, g_hbm, live_ref, master_ref, first_ref, second_ref,
     new_master_ref, new_first_ref, new_second_ref, w_ref,
-    h_buf, ht, gb, xs, xr, s_buf, m1s, m1r, m2s, m2r, part, keep2, p2s, p2r, p3s, p3r,
+    h_buf, ht, gb, theirs, xs, xr, s_buf, m1s, m1r, m2s, m2r, part, keep2, p2s, p2r, p3s, p3r,
     c1s, c1r, rc, c2s, c2r, kc, c3s, c3r, grad, w_buf,
     h_sem, gl_sem, xs_sem, xr_sem, one_s, one_r, two_s, two_r, p2_s, p2_r, p3_s, p3_r,
     c1_s, c1_r, c2_s, c2_r, c3_s, c3_r, wz_s, wz_r, wy_s, wy_r, wc_s, wc_r,
@@ -77,6 +78,7 @@
     to_y = [(lax.div(at, 2) * 16 + lax.rem(node, 16), lax.rem(at, 2) * 4 + x) for at in ys_at]
     z_nodes = [[half * 16 + at * 2 + core for at in zs_at] for half in (yh, 1 - yh)]
     to_z = [(at, local) for at in z_nodes[0]]
+    to_far = [(z_nodes[1][i], local) for i in FAR]
     to_core = (node + 1 - 2 * core, local)
 
     def remote(src, dst, send, recv, to):
@@ -96,8 +98,8 @@
             gl_sem.at[k],
         )
 
-    def swap(k):
-        return remote(xs.at[k], xr.at[k], xs_sem, xr_sem.at[k], to_core)
+    def swap(k, block):
+        return remote(xs.at[k, block], xr.at[k, block], xs_sem, xr_sem.at[k], to_core)
 
     def wait_for(ref, sem):
         pltpu.make_async_copy(ref, ref, sem).wait()
@@ -106,7 +108,7 @@
         return pltpu.make_async_copy(h_hbm.at[:, pl.ds(j * 256, 256)], h_buf.at[:, pl.ds(j * 256, 256)], h_sem.at[j])
 
     barrier = pltpu.get_barrier_semaphore()
-    partners = [*to_x[1:], *to_y[1:], *to_z[1:], to_core]
+    partners = [*to_x[1:], *to_y[1:], *to_z[1:], to_core, *to_far]
     for partner in partners:
         pl.semaphore_signal(barrier, inc=1, device_id=partner, device_id_type=MESH)
     for j in range(4):
@@ -294,16 +296,23 @@
         product = jnp.dot(ht[...], gb[k], preferred_element_type=F32)
         for half in range(2):
             s_buf[k, half] = product[:, half * BLK : half * BLK + BLK]
-            xs[k, half] = product[:, (2 + half) * BLK : (3 + half) * BLK]
-        swap(k).start()
+            theirs[half] = product[:, (2 + half) * BLK : (3 + half) * BLK]
+
+        def quantize(block, carry):
+            send_codes(lambda i: theirs[i // 8, rows_of(block, 16 * (i % 8)), :], 16, xs.at[k, block])
+            swap(k, block).start()
+            return carry
+
+        lax.fori_loop(0, 8, quantize, 0)
 
     def add_core(k):
-        swap(k).wait_recv()
+        wait_for(xr.at[k], xr_sem.at[k])
 
         def add(block, carry):
-            rows = rows_of(block, 0, BLK)
-            for half in range(2):
-                s_buf[k, half, rows, :] += xr[k, half, rows, :]
+            message = xr.at[k, block]
+            unit = unit_of(message)
+            for i in range(16):
+                s_buf[k, i // 8, rows_of(block, 16 * (i % 8)), :] += decode(message, i, unit)
             return carry
 
         lax.fori_loop(0, 8, add, 0)
@@ -359,6 +368,9 @@
         at = w_at(-j % NZ)
         return remote(at, at, wy_s, wy_r.at[j], to_y[2])
 
+    def w_far(i):
+        return remote(w_at(), w_at(), wy_s, wy_r.at[FAR[i]], to_far[i])
+
     def w_c(j, other):
         at = w_at(-j % NZ, other)
         return remote(at, at, wc_s, wc_r, to_core)
@@ -366,10 +378,15 @@
     w_at()[...] = new_master.astype(BF16)
 
     def spread(j):
-        w_y(j).start()
+        if j not in FAR:
+            w_y(j).start()
         w_c(j, 0).start()
 
-    for i in (2, 3, 0, 1):
+    for i in (2, 3):
+        w_z(i).start()
+    for i in range(3):
+        w_far(i).start()
+    for i in (0, 1):
         w_z(i).start()
     spread(0)
     new_master_ref[...] = new_master
@@ -419,7 +436,7 @@
             pltpu.VMEM((TOK, FFW), BF16),
             pltpu.VMEM((FFW, TOK), BF16),
             pltpu.VMEM((8, TOK, 4 * BLK), BF16),
-            pltpu.VMEM((8, 2, FFW, BLK), F32), pltpu.VMEM((8, 2, FFW, BLK), F32), pltpu.VMEM((8, 2, FFW, BLK), F32),
+            pltpu.VMEM((2, FFW, BLK), F32), tiles(8, 8, 17), tiles(8, 8, 17), pltpu.VMEM((8, 2, FFW, BLK), F32),
             tiles(8, 2, 2, 13), tiles(8, 2, 2, 13), tiles(8, 2, 2, 7), tiles(8, 2, 2, 7),
             tiles(2, 4, 6, kind=F32), tiles(4, 2, 6, kind=F32),
             tiles(4, 2, 3, 7), tiles(4, 2, 3, 7), tiles(7, 7), tiles(7, 7),

time: 64.9 us -> 64.1 us (0.988)
  Pallas kernels: 63.5 us -> 62.6 us
    pallas_call x1, Pallas kernels: 62.4 us -> 61.6 us  [body(): pl.pallas_call(kernel, out_shape=(block, block, block, pltpu.VMEM((BLK, D...]
where the time goes in v4:
time: 64.1 us; the launch traced here: 63.9 us
  Pallas kernels  62.6 us (98%)
  between operations  1.29 us (2%)
    pallas_call x1, Pallas kernels, body(): pl.pallas_call(kernel, out_shape=(block, block, block, pltpu.VMEM((BLK, D...  61.6 us

profile of v4, /device:TPU:1, one launch (start us, length us, event | category | flops | bytes accessed | tf_op | source)
XLA Modules:
  0.0 63.9 jit_solution(6784125003534685872)
XLA Ops:
  1.3 61.6 %grad_update.1 = (f32[128,128]{1,0:T(8,128)S(1)}, f32[128,128]{1,0:T(8,128)S(1)}, f32[128,128]{1,0:T(8,128)S(1)}, bf16[128,4096]{1,0:T(8,128)(2,1)S(1)}) custom-call(bf16[1024,1024]{1,0:T(8,128)(2,1)} %h_hbm.1, bf16[1024,4096]{1,0:T(8,128)(2,1)} %g_hbm.1, s32[1,1]{1,0:T(1,128)S(6)} %copy.10.live_ref, f32[128,128]{1,0:T(8,128)} %master_ref.1, ...), custom_call_target="tpu_custom_call" | custom-call | flops 8589934592 | bytes 12582912 | tf_op jit(solution)/shard_map/grad_update/pallas_call | solution.py:430
  62.8 1.1 %hand_out.1 = (f32[128,128]{1,0:T(8,128)}, f32[128,128]{1,0:T(8,128)}, f32[128,128]{1,0:T(8,128)}, bf16[128,4096]{1,0:T(8,128)(2,1)}) custom-call(f32[128,128]{1,0:T(8,128)S(1)} %get-tuple-element.8.refs_0_, f32[128,128]{1,0:T(8,128)S(1)} %get-tuple-element.9.refs_1_, f32[128,128]{1,0:T(8,128)S(1)} %get-tuple-element.10.refs_2_, ...), custom_call_target="tpu_custom_call" | custom-call | tf_op jit(solution)/shard_map/hand_out/pallas_call | solution.py:459
